TPU v7x, 256 devices: a whole 4x4x8 slice. The times are simulated.
256 devices in a mesh: dp: 2 (over core), ctx: 32 (over x, z), tp: 4 (over y).
Axes of the slice: x: 4, y: 4, z: 8, core: 2. Of those that a mesh axis runs over, the one named last changes fastest.
Arguments:
- queries: bfloat16 [8192, 4096], P(('dp', 'ctx'), 'tp'), parts along dimension 0, may hold values from -8 to 8
- keys: bfloat16 [64, 1601, 512], P(('dp', 'ctx'), None, 'tp'), parts along dimension 0, may hold values from -6 to 6
- values: bfloat16 [64, 1601, 512], P(('dp', 'ctx'), None, 'tp'), parts along dimension 0, may hold values from -6 to 6
- refs: int32 [64, 4], P(('dp', 'ctx')), parts along dimension 0, may hold values from -1 to 31, as said below
- upstream: bfloat16 [8192, 4096], P(('dp', 'ctx'), 'tp'), parts along dimension 0, may hold values from -6 to 6
Outputs:
- attended: bfloat16 [8192, 4096], P(('dp', 'ctx'), 'tp'), parts along dimension 0
- query_grad: bfloat16 [8192, 4096], P(('dp', 'ctx'), 'tp'), parts along dimension 0
- key_grad: float32 [64, 1601, 512], P(('dp', 'ctx'), None, 'tp'), parts along dimension 0
- value_grad: float32 [64, 1601, 512], P(('dp', 'ctx'), None, 'tp'), parts along dimension 0
There are 2 independent parts, one for each index of `dp`. A program takes and returns all parts, laid end to end along the dimension named above; each array names one. Nothing has to cross between parts.
Inputs may be any that keep to these rules, and one draw needn't show every extreme that they name: `refs`: row b lists the images that text block b attends: 1 to 4 distinct ids first, then -1 in the unused slots. Every id i satisfies (b - 3) <= i < (b + 1), so images are held in document order, 1 to each device of ctx. Block 0 names one image; the last block names 4, image 32 - 1 among them.
All inputs are finite; a program needn't handle non-finite values.
Results may differ from a plain program's by a relative error of at most 0.0081.
Values may be sent and summed in bfloat16 or wider, within the bound.
A program may use at most 64 MiB of HBM per device.

v0:
```python
import jax
import jax.numpy as jnp
from jax import lax
from jax.sharding import PartitionSpec as P

HEADS = 32
KVH = 4
HD = 128
BLOCK = 128
REACH = 3


head_step = 4
far_below = -1e30


def from_behind(block, axis, distance):
    devices = range(lax.axis_size(axis))
    route = [(i - distance, i) for i in devices if i - distance in devices]
    return lax.ppermute(block, axis, route)


def head_scores(q_part, k_head):
    score_scale = k_head.shape[1] ** (-0.5)
    per_head = q_part.reshape(q_part.shape[0], head_step, k_head.shape[1])
    return (
        jnp.einsum("thd,jd->htj", per_head, k_head, preferred_element_type=jnp.float32)
        * score_scale
    )


def head_slices(local_heads):
    group_size = HEADS // KVH
    spans = []
    for first_head in range(0, local_heads, head_step):
        kv_index = first_head // group_size
        spans.append(
            (first_head, first_head * HD, (first_head + head_step) * HD, kv_index * HD, kv_index)
        )
    return spans


def pair_stats(q_block, k_img):
    maxima = []
    totals = []
    for first_head, q_low, q_high, k_low, kv_index in head_slices(q_block.shape[1] // HD):
        scores = head_scores(q_block[:, q_low:q_high], k_img[:, k_low : k_low + HD])
        highest = jnp.max(scores, axis=2)
        maxima.append(highest)
        totals.append(jnp.sum(jnp.exp(scores - highest[:, :, None]), axis=2))
    return (jnp.concatenate(maxima, 0), jnp.concatenate(totals, 0))


def pair_out(q_block, k_img, v_img, log_total):
    pieces = []
    for first_head, q_low, q_high, k_low, kv_index in head_slices(q_block.shape[1] // HD):
        scores = head_scores(q_block[:, q_low:q_high], k_img[:, k_low : k_low + HD])
        weights = jnp.exp(scores - log_total[first_head : first_head + head_step, :, None]).astype(
            jnp.bfloat16
        )
        mixed_rows = jnp.einsum(
            "htj,jd->thd", weights, v_img[:, k_low : k_low + HD], preferred_element_type=jnp.float32
        )
        pieces.append(mixed_rows.reshape(mixed_rows.shape[0], head_step * HD))
    return jnp.concatenate(pieces, 1)


def pair_back(q_block, g_block, k_img, v_img, log_total, deltas):
    score_scale = HD ** (-0.5)
    kv_count = k_img.shape[1] // HD
    key_parts = [jnp.zeros((k_img.shape[0], HD), jnp.float32) for kv_slot in range(kv_count)]
    value_parts = [jnp.zeros((k_img.shape[0], HD), jnp.float32) for kv_slot in range(kv_count)]
    query_parts = []
    for first_head, q_low, q_high, k_low, kv_index in head_slices(q_block.shape[1] // HD):
        k_head = k_img[:, k_low : k_low + HD]
        v_head = v_img[:, k_low : k_low + HD]
        q_rows = q_block[:, q_low:q_high].reshape(q_block.shape[0], head_step, HD)
        upward = g_block[:, q_low:q_high].reshape(q_block.shape[0], head_step, HD)
        scores = head_scores(q_block[:, q_low:q_high], k_head)
        p_full = jnp.exp(scores - log_total[first_head : first_head + head_step, :, None])
        weights = p_full.astype(jnp.bfloat16)
        dweights = jnp.einsum("thd,jd->htj", upward, v_head, preferred_element_type=jnp.float32)
        dscores = (
            p_full * (dweights - deltas[first_head : first_head + head_step, :, None])
        ).astype(jnp.bfloat16)
        q_part = (
            jnp.einsum("htj,jd->thd", dscores, k_head, preferred_element_type=jnp.float32)
            * score_scale
        )
        query_parts.append(q_part.reshape(q_block.shape[0], head_step * HD))
        key_parts[kv_index] = (
            key_parts[kv_index]
            + jnp.einsum("htj,thd->jd", dscores, q_rows, preferred_element_type=jnp.float32)
            * score_scale
        )
        value_parts[kv_index] = value_parts[kv_index] + jnp.einsum(
            "htj,thd->jd", weights, upward, preferred_element_type=jnp.float32
        )
    return (
        jnp.concatenate(query_parts, 1),
        jnp.concatenate(key_parts, 1),
        jnp.concatenate(value_parts, 1),
    )


def merge_stats(maxima, totals):
    highest = jnp.max(maxima, axis=0)
    return highest + jnp.log(jnp.sum(totals * jnp.exp(maxima - highest[None]), axis=0))


def block_forward(q_block, use_row, cand_keys, cand_values):
    local_heads = q_block.shape[1] // HD
    empty_stats = (
        jnp.full((local_heads, q_block.shape[0]), far_below, jnp.float32),
        jnp.zeros((local_heads, q_block.shape[0]), jnp.float32),
    )

    def one_stats(operands):
        k_img, is_used = operands
        return lax.cond(is_used, lambda: pair_stats(q_block, k_img), lambda: empty_stats)

    maxima, totals = lax.map(one_stats, (cand_keys, use_row))
    log_total = merge_stats(maxima, totals)
    blank_rows = jnp.zeros(q_block.shape, jnp.float32)

    def add_out(running, operands):
        k_img, v_img, is_used = operands
        return (
            running
            + lax.cond(
                is_used, lambda: pair_out(q_block, k_img, v_img, log_total), lambda: blank_rows
            ),
            None,
        )

    attended, unused = lax.scan(add_out, blank_rows, (cand_keys, cand_values, use_row))
    return (attended.astype(jnp.bfloat16), log_total)


def pairs_backward(block_queries, block_grads, log_totals, deltas, uses, img_keys, img_values):
    zero_rows = jnp.zeros(block_queries.shape[1:], jnp.float32)
    zero_tile = jnp.zeros(img_keys.shape[1:], jnp.float32)

    def block_step(running, operands):
        q_block, g_block, log_total, row_deltas, use_row = operands

        def pair_step(q_total, pair_operands):
            k_img, v_img, is_used = pair_operands
            q_part, k_part, v_part = lax.cond(
                is_used,
                lambda: pair_back(q_block, g_block, k_img, v_img, log_total, row_deltas),
                lambda: (zero_rows, zero_tile, zero_tile),
            )
            return (q_total + q_part, (k_part, v_part))

        q_grad, tile_parts = lax.scan(pair_step, zero_rows, (img_keys, img_values, use_row))
        return ((running[0] + tile_parts[0], running[1] + tile_parts[1]), q_grad)

    zero_tiles = jnp.zeros(img_keys.shape, jnp.float32)
    tile_totals, query_grads = lax.scan(
        block_step, (zero_tiles, zero_tiles), (block_queries, block_grads, log_totals, deltas, uses)
    )
    return (query_grads, tile_totals[0], tile_totals[1])


def on_device(queries, keys, values, refs, upstream):
    blocks_here = queries.shape[0] // BLOCK
    images_here = keys.shape[0]
    local_heads = queries.shape[1] // HD
    here = lax.axis_index("ctx")
    tile_keys = [keys]
    tile_values = [values]
    for distance in range(1, REACH + 1):
        far_keys, far_values = from_behind((keys, values), "ctx", distance)
        tile_keys.append(far_keys)
        tile_values.append(far_values)
    cand_keys = jnp.concatenate(tile_keys, 0)
    cand_values = jnp.concatenate(tile_values, 0)
    owners = here - jnp.repeat(jnp.arange(REACH + 1, dtype=jnp.int32), images_here)
    cand_ids = owners * images_here + jnp.tile(jnp.arange(images_here, dtype=jnp.int32), REACH + 1)
    uses = jnp.any(refs[:, None, :] == cand_ids[None, :, None], axis=2) & (owners >= 0)[None, :]
    block_queries = queries.reshape(blocks_here, BLOCK, queries.shape[1])
    block_grads = upstream.reshape(blocks_here, BLOCK, upstream.shape[1])
    attended, log_totals = lax.map(
        lambda operands: block_forward(operands[0], operands[1], cand_keys, cand_values),
        (block_queries, uses),
    )
    products = block_grads.astype(jnp.float32) * attended.astype(jnp.float32)
    deltas = jnp.sum(products.reshape(blocks_here, BLOCK, local_heads, HD), axis=3).transpose(
        0, 2, 1
    )
    query_grads, cand_kgrads, cand_vgrads = pairs_backward(
        block_queries, block_grads, log_totals, deltas, uses, cand_keys, cand_values
    )
    key_grads = cand_kgrads[:images_here]
    value_grads = cand_vgrads[:images_here]
    for distance in range(1, REACH + 1):
        lower_edge = distance * images_here
        back_keys, back_values = (
            from_behind(
                cand_kgrads[lower_edge : lower_edge + images_here].astype(jnp.bfloat16),
                "ctx",
                -distance,
            ).astype(jnp.float32),
            from_behind(
                cand_vgrads[lower_edge : lower_edge + images_here].astype(jnp.bfloat16),
                "ctx",
                -distance,
            ).astype(jnp.float32),
        )
        key_grads = key_grads + back_keys
        value_grads = value_grads + back_values
    attended_out = attended.reshape(queries.shape)
    query_out = query_grads.reshape(queries.shape).astype(jnp.bfloat16)
    return (attended_out, query_out, key_grads, value_grads)


def solution(mesh):
    return jax.shard_map(
        on_device,
        mesh=mesh,
        in_specs=(
            P(("dp", "ctx"), "tp"),
            P(("dp", "ctx"), None, "tp"),
            P(("dp", "ctx"), None, "tp"),
            P(("dp", "ctx"), None),
            P(("dp", "ctx"), "tp"),
        ),
        out_specs=(
            P(("dp", "ctx"), "tp"),
            P(("dp", "ctx"), "tp"),
            P(("dp", "ctx"), None, "tp"),
            P(("dp", "ctx"), None, "tp"),
        ),
        check_vma=False,
    )
```

profile of v0, /device:TPU:166, one launch (start us, length us, event | category | flops | bytes accessed | tf_op | source)
XLA Modules:
  0.0 623.5 jit_solution(10339909164464858789)
XLA Ops:
  0.7 3.5 collective-permute-start.1
  16.8 17.7 %collective-permute-done = bf16[1,1601,128]{2,1,0:T(8,128)(2,1)} collective-permute-done((bf16[1,1601,128]{2,1,0:T(8,128)(2,1)}, bf16[1,1601,128]{2,1,0:T(8,128)(2,1)}, u32[]{:S(2)}, u32[]{:S(2)}) %collective-permute-start) | collective-permute-done | bytes 409888 | tf_op jit(solution)/shard_map/ppermute | solution.py:20
  37.0 42.8 %collective-permute-done.2 = bf16[1,1601,128]{2,1,0:T(8,128)(2,1)} collective-permute-done((bf16[1,1601,128]{2,1,0:T(8,128)(2,1)}, bf16[1,1601,128]{2,1,0:T(8,128)(2,1)}, u32[]{:S(2)}, u32[]{:S(2)}) %collective-permute-start.2) | collective-permute-done | bytes 409888 | tf_op jit(solution)/shard_map/ppermute | solution.py:20
  80.9 15.8 %while.61 = (s32[]{:T(128)}, f32[4,8,128]{2,1,0:T(8,128)S(1)}, f32[4,8,128]{2,1,0:T(8,128)S(1)}, pred[4]{0:T(512)(128)(4,1)}, bf16[4,1601,128]{2,1,0:T(8,128)(2,...) while((s32[]{:T(128)}, f32[4,8,128]{2,1,0:T(8,128)S(1)}, f32[4,8,128]{2,1,0:T(8,128)S(1)}, ...), condition=%wide.region_8.9_spmd, body=%wide.region_1.8_spmd.sunk | while | flops 426250240 | bytes 14770324 | solution.py:122
  82.6 2.1 conditional.8
  86.6 2.1 conditional.8
  90.5 2.1 conditional.8
  94.5 2.1 conditional.8
  100.9 13.0 %collective-permute-done.5 = bf16[1,1601,128]{2,1,0:T(8,128)(2,1)} collective-permute-done((bf16[1,1601,128]{2,1,0:T(8,128)(2,1)S(1)}, bf16[1,1601,128]{2,1,0:T(8,128)(2,1)}, u32[]{:S(2)}, u32[]{:S(2)}) %collective-permute-start.5) | collective-permute-done | bytes 409888 | tf_op jit(solution)/shard_map/ppermute | solution.py:20
  115.8 27.2 %while.62 = (s32[]{:T(128)}, f32[128,1024]{0,1:T(8,128)S(1)}, pred[4]{0:T(512)(128)(4,1)}, bf16[4,1601,128]{2,1,0:T(8,128)(2,1)S(1)}, bf16[128,1024]{0,1:T(8,128...) while((s32[]{:T(128)}, f32[128,1024]{0,1:T(8,128)S(1)}, ...), condition=%wide.region_14.15_spmd.clone, body=%wide.region_11.14_spmd.clone.sunk | while | flops 844696576 | bytes 5593258 | solution.py:136
  117.6 4.8 conditional.9
  124.4 4.8 conditional.9
  131.2 4.8 conditional.9
  134.0 2.0 fusion.15
  138.0 4.8 conditional.9
  140.8 2.0 fusion.15
  145.8 273.7 %while.63 = (s32[]{:T(128)}, f32[128,1024]{0,1:T(8,128)}, f32[4,1601,128]{2,0,1:T(4,128)}, f32[4,1601,128]{2,0,1:T(4,128)}, pred[4]{0:T(512)(128)(4,1)}, /*index...) while((s32[]{:T(128)}, f32[128,1024]{0,1:T(8,128)}, ...), condition=%wide.region_19.20_spmd.clone, body=%wide.region_16.19_spmd.clone.sunk | while | flops 2109438336 | bytes 58602816 | solution.py:156
  147.7 8.5 %conditional.10 = (f32[128,1024]{0,1:T(8,128)S(1)}, f32[1,1601,128]{2,1,0:T(8,128)S(1)}, f32[1,1601,128]{2,1,0:T(8,128)S(1)}) conditional(s32[]{:T(128)} %bitcast.169, () %tuple.145, (bf16[4,1601,128]{2,1,0:T(8,128)(2,1)S(1)}, s32[]{:T(128)}, bf16[128,1024]{0,1:T(8,128)(2,1)S(1)}, f32[8,128]{1,0:T(8,128)}, bf16[4,1601,128]{2,1,0:T(8,128)(2,1)}, ...), branch_computations={%region_17.17_spmd, %region_18.18_spmd} | conditional | flops 2109176192 | bytes 47193164 | solution.py:149
  157.1 5.8 copy.121
  162.9 5.8 copy.122
  168.7 22.4 %dynamic_update_slice.32 = f32[4,1601,128]{2,0,1:T(4,128)} dynamic-update-slice(f32[4,1601,128]{2,0,1:T(4,128)} %get-tuple-element.789, f32[1,1601,128]{2,0,1:T(1,128)} %copy.122, s32[]{:T(128)} %copy.164, s32[]{:T(128)} %constant.118.clone.1..sunk.1, s32[]{:T(128)} %constant.118.clone.1..sunk.1) | dynamic-update-slice | bytes 1639428 | tf_op jit(solution)/shard_map/while/body/eval_jaxpr/while/body/jit(dynamic_update_index_in_dim)/dynamic_update_slice | solution.py:156
  191.1 22.4 %dynamic_update_slice.31 = f32[4,1601,128]{2,0,1:T(4,128)} dynamic-update-slice(f32[4,1601,128]{2,0,1:T(4,128)} %get-tuple-element.788, f32[1,1601,128]{2,0,1:T(1,128)S(1)} %copy-done, s32[]{:T(128)} %copy.164, s32[]{:T(128)} %constant.118.clone.1..sunk.1, s32[]{:T(128)} %constant.118.clone.1..sunk.1) | dynamic-update-slice | bytes 1639428 | tf_op jit(solution)/shard_map/while/body/eval_jaxpr/while/body/jit(dynamic_update_index_in_dim)/dynamic_update_slice | solution.py:156
  215.3 8.5 %conditional.10 = (f32[128,1024]{0,1:T(8,128)S(1)}, f32[1,1601,128]{2,1,0:T(8,128)S(1)}, f32[1,1601,128]{2,1,0:T(8,128)S(1)}) conditional(s32[]{:T(128)} %bitcast.169, () %tuple.145, (bf16[4,1601,128]{2,1,0:T(8,128)(2,1)S(1)}, s32[]{:T(128)}, bf16[128,1024]{0,1:T(8,128)(2,1)S(1)}, f32[8,128]{1,0:T(8,128)}, bf16[4,1601,128]{2,1,0:T(8,128)(2,1)}, ...), branch_computations={%region_17.17_spmd, %region_18.18_spmd} | conditional | flops 2109176192 | bytes 47193164 | solution.py:149
  225.7 5.8 copy.121
  231.6 5.8 copy.122
  237.4 22.4 %dynamic_update_slice.32 = f32[4,1601,128]{2,0,1:T(4,128)} dynamic-update-slice(f32[4,1601,128]{2,0,1:T(4,128)} %get-tuple-element.789, f32[1,1601,128]{2,0,1:T(1,128)} %copy.122, s32[]{:T(128)} %copy.164, s32[]{:T(128)} %constant.118.clone.1..sunk.1, s32[]{:T(128)} %constant.118.clone.1..sunk.1) | dynamic-update-slice | bytes 1639428 | tf_op jit(solution)/shard_map/while/body/eval_jaxpr/while/body/jit(dynamic_update_index_in_dim)/dynamic_update_slice | solution.py:156
  259.8 22.4 %dynamic_update_slice.31 = f32[4,1601,128]{2,0,1:T(4,128)} dynamic-update-slice(f32[4,1601,128]{2,0,1:T(4,128)} %get-tuple-element.788, f32[1,1601,128]{2,0,1:T(1,128)S(1)} %copy-done, s32[]{:T(128)} %copy.164, s32[]{:T(128)} %constant.118.clone.1..sunk.1, s32[]{:T(128)} %constant.118.clone.1..sunk.1) | dynamic-update-slice | bytes 1639428 | tf_op jit(solution)/shard_map/while/body/eval_jaxpr/while/body/jit(dynamic_update_index_in_dim)/dynamic_update_slice | solution.py:156
  284.0 8.5 %conditional.10 = (f32[128,1024]{0,1:T(8,128)S(1)}, f32[1,1601,128]{2,1,0:T(8,128)S(1)}, f32[1,1601,128]{2,1,0:T(8,128)S(1)}) conditional(s32[]{:T(128)} %bitcast.169, () %tuple.145, (bf16[4,1601,128]{2,1,0:T(8,128)(2,1)S(1)}, s32[]{:T(128)}, bf16[128,1024]{0,1:T(8,128)(2,1)S(1)}, f32[8,128]{1,0:T(8,128)}, bf16[4,1601,128]{2,1,0:T(8,128)(2,1)}, ...), branch_computations={%region_17.17_spmd, %region_18.18_spmd} | conditional | flops 2109176192 | bytes 47193164 | solution.py:149
  294.4 5.8 copy.121
  300.3 5.8 copy.122
  306.1 22.4 %dynamic_update_slice.32 = f32[4,1601,128]{2,0,1:T(4,128)} dynamic-update-slice(f32[4,1601,128]{2,0,1:T(4,128)} %get-tuple-element.789, f32[1,1601,128]{2,0,1:T(1,128)} %copy.122, s32[]{:T(128)} %copy.164, s32[]{:T(128)} %constant.118.clone.1..sunk.1, s32[]{:T(128)} %constant.118.clone.1..sunk.1) | dynamic-update-slice | bytes 1639428 | tf_op jit(solution)/shard_map/while/body/eval_jaxpr/while/body/jit(dynamic_update_index_in_dim)/dynamic_update_slice | solution.py:156
  328.5 22.4 %dynamic_update_slice.31 = f32[4,1601,128]{2,0,1:T(4,128)} dynamic-update-slice(f32[4,1601,128]{2,0,1:T(4,128)} %get-tuple-element.788, f32[1,1601,128]{2,0,1:T(1,128)S(1)} %copy-done, s32[]{:T(128)} %copy.164, s32[]{:T(128)} %constant.118.clone.1..sunk.1, s32[]{:T(128)} %constant.118.clone.1..sunk.1) | dynamic-update-slice | bytes 1639428 | tf_op jit(solution)/shard_map/while/body/eval_jaxpr/while/body/jit(dynamic_update_index_in_dim)/dynamic_update_slice | solution.py:156
  352.7 8.5 %conditional.10 = (f32[128,1024]{0,1:T(8,128)S(1)}, f32[1,1601,128]{2,1,0:T(8,128)S(1)}, f32[1,1601,128]{2,1,0:T(8,128)S(1)}) conditional(s32[]{:T(128)} %bitcast.169, () %tuple.145, (bf16[4,1601,128]{2,1,0:T(8,128)(2,1)S(1)}, s32[]{:T(128)}, bf16[128,1024]{0,1:T(8,128)(2,1)S(1)}, f32[8,128]{1,0:T(8,128)}, bf16[4,1601,128]{2,1,0:T(8,128)(2,1)}, ...), branch_computations={%region_17.17_spmd, %region_18.18_spmd} | conditional | flops 2109176192 | bytes 47193164 | solution.py:149
  363.1 5.8 copy.121
  369.0 5.8 copy.122
  374.8 22.4 %dynamic_update_slice.32 = f32[4,1601,128]{2,0,1:T(4,128)} dynamic-update-slice(f32[4,1601,128]{2,0,1:T(4,128)} %get-tuple-element.789, f32[1,1601,128]{2,0,1:T(1,128)} %copy.122, s32[]{:T(128)} %copy.164, s32[]{:T(128)} %constant.118.clone.1..sunk.1, s32[]{:T(128)} %constant.118.clone.1..sunk.1) | dynamic-update-slice | bytes 1639428 | tf_op jit(solution)/shard_map/while/body/eval_jaxpr/while/body/jit(dynamic_update_index_in_dim)/dynamic_update_slice | solution.py:156
  397.2 22.4 %dynamic_update_slice.31 = f32[4,1601,128]{2,0,1:T(4,128)} dynamic-update-slice(f32[4,1601,128]{2,0,1:T(4,128)} %get-tuple-element.788, f32[1,1601,128]{2,0,1:T(1,128)S(1)} %copy-done, s32[]{:T(128)} %copy.164, s32[]{:T(128)} %constant.118.clone.1..sunk.1, s32[]{:T(128)} %constant.118.clone.1..sunk.1) | dynamic-update-slice | bytes 1639428 | tf_op jit(solution)/shard_map/while/body/eval_jaxpr/while/body/jit(dynamic_update_index_in_dim)/dynamic_update_slice | solution.py:156
  421.4 2.2 convert.14
  423.7 2.2 fusion.72
  431.7 2.2 fusion.73
  437.2 17.1 %collective-permute-done.9 = bf16[1,1601,128]{2,0,1:T(2,128)(2,1)S(1)} collective-permute-done((bf16[1,1601,128]{2,0,1:T(2,128)(2,1)S(1)}, bf16[1,1601,128]{2,0,1:T(2,128)(2,1)S(1)}, u32[]{:S(2)}, u32[]{:S(2)}) %collective-permute-start.9) | collective-permute-done | bytes 409888 | tf_op jit(solution)/shard_map/ppermute | solution.py:20
  456.3 48.6 %collective-permute-done.11 = bf16[1,1601,128]{2,0,1:T(2,128)(2,1)S(1)} collective-permute-done((bf16[1,1601,128]{2,0,1:T(2,128)(2,1)S(1)}, bf16[1,1601,128]{2,0,1:T(2,128)(2,1)S(1)}, u32[]{:S(2)}, u32[]{:S(2)}) %collective-permute-start.11) | collective-permute-done | bytes 409888 | tf_op jit(solution)/shard_map/ppermute | solution.py:20
  504.9 29.0 %collective-permute-done.10 = bf16[1,1601,128]{2,0,1:T(2,128)(2,1)S(1)} collective-permute-done((bf16[1,1601,128]{2,0,1:T(2,128)(2,1)S(1)}, bf16[1,1601,128]{2,0,1:T(2,128)(2,1)S(1)}, u32[]{:S(2)}, u32[]{:S(2)}) %collective-permute-start.10) | collective-permute-done | bytes 409888 | tf_op jit(solution)/shard_map/ppermute | solution.py:20
  533.9 4.4 convert_add_fusion
  538.2 14.2 %collective-permute-done.6 = bf16[1,1601,128]{2,0,1:T(2,128)(2,1)S(1)} collective-permute-done((bf16[1,1601,128]{2,0,1:T(2,128)(2,1)S(1)}, bf16[1,1601,128]{2,0,1:T(2,128)(2,1)S(1)}, u32[]{:S(2)}, u32[]{:S(2)}) %collective-permute-start.6) | collective-permute-done | bytes 409888 | tf_op jit(solution)/shard_map/ppermute | solution.py:20
  552.4 20.4 %collective-permute-done.8 = bf16[1,1601,128]{2,0,1:T(2,128)(2,1)S(1)} collective-permute-done((bf16[1,1601,128]{2,0,1:T(2,128)(2,1)S(1)}, bf16[1,1601,128]{2,0,1:T(2,128)(2,1)S(1)}, u32[]{:S(2)}, u32[]{:S(2)}) %collective-permute-start.8) | collective-permute-done | bytes 409888 | tf_op jit(solution)/shard_map/ppermute | solution.py:20
  572.8 47.7 %collective-permute-done.7 = bf16[1,1601,128]{2,0,1:T(2,128)(2,1)S(1)} collective-permute-done((bf16[1,1601,128]{2,0,1:T(2,128)(2,1)S(1)}, bf16[1,1601,128]{2,0,1:T(2,128)(2,1)S(1)}, u32[]{:S(2)}, u32[]{:S(2)}) %collective-permute-start.7) | collective-permute-done | bytes 409888 | tf_op jit(solution)/shard_map/ppermute | solution.py:20
  620.6 2.9 convert_add_fusion.1
  (185 shorter events, 116.4 us)
Async XLA Ops:
  0.6 14.9 %copy-start.4 = (bf16[1,1601,128]{2,1,0:T(8,128)(2,1)S(1)}, bf16[1,1601,128]{2,1,0:T(8,128)(2,1)}, u32[]{:S(2)}) copy-start(bf16[1,1601,128]{2,1,0:T(8,128)(2,1)} %param.19) | copy-start | bytes 1229572
  0.6 14.7 %copy-start.5 = (s32[1,4]{1,0:T(1,128)S(1)}, s32[1,4]{1,0:T(1,128)}, u32[]{:S(2)}) copy-start(s32[1,4]{1,0:T(1,128)} %param.20) | copy-start | bytes 52
  0.7 36.3 %collective-permute-start.1 = (bf16[1,1601,128]{2,1,0:T(8,128)(2,1)}, bf16[1,1601,128]{2,1,0:T(8,128)(2,1)S(1)}, u32[]{:S(2)}, u32[]{:S(2)}) collective-permute-start(bf16[1,1601,128]{2,1,0:T(8,128)(2,1)} %param.18), channel_id=1, source_target_pairs={{0,8},{4,12},{8,16},{12,20},{16,24},{20,28},{24,32},{28,36},{32,40... | collective-permute-start | bytes 1229576 | tf_op jit(solution)/shard_map/ppermute | solution.py:20
  4.2 30.4 %collective-permute-start = (bf16[1,1601,128]{2,1,0:T(8,128)(2,1)}, bf16[1,1601,128]{2,1,0:T(8,128)(2,1)}, u32[]{:S(2)}, u32[]{:S(2)}) collective-permute-start(bf16[1,1601,128]{2,1,0:T(8,128)(2,1)} %param.18), channel_id=1, source_target_pairs={{0,4},{4,8},{8,12},{12,16},{16,20},{20,24},{24,28},{28,32},{32,36}... | collective-permute-start | bytes 1229576 | tf_op jit(solution)/shard_map/ppermute | solution.py:20
  6.1 73.7 %collective-permute-start.2 = (bf16[1,1601,128]{2,1,0:T(8,128)(2,1)}, bf16[1,1601,128]{2,1,0:T(8,128)(2,1)}, u32[]{:S(2)}, u32[]{:S(2)}) collective-permute-start(bf16[1,1601,128]{2,1,0:T(8,128)(2,1)} %param.18), channel_id=1, source_target_pairs={{0,12},{4,16},{8,20},{12,24},{16,28},{20,32},{24,36},{28,40},{32,4... | collective-permute-start | bytes 1229576 | tf_op jit(solution)/shard_map/ppermute | solution.py:20
  7.4 91.7 %collective-permute-start.4 = (bf16[1,1601,128]{2,1,0:T(8,128)(2,1)}, bf16[1,1601,128]{2,1,0:T(8,128)(2,1)}, u32[]{:S(2)}, u32[]{:S(2)}) collective-permute-start(bf16[1,1601,128]{2,1,0:T(8,128)(2,1)} %param.19), channel_id=1, source_target_pairs={{0,8},{4,12},{8,16},{12,20},{16,24},{20,28},{24,32},{28,36},{32,40... | collective-permute-start | bytes 1229576 | tf_op jit(solution)/shard_map/ppermute | solution.py:20
  9.3 87.4 %collective-permute-start.3 = (bf16[1,1601,128]{2,1,0:T(8,128)(2,1)}, bf16[1,1601,128]{2,1,0:T(8,128)(2,1)}, u32[]{:S(2)}, u32[]{:S(2)}) collective-permute-start(bf16[1,1601,128]{2,1,0:T(8,128)(2,1)} %param.19), channel_id=1, source_target_pairs={{0,4},{4,8},{8,12},{12,16},{16,20},{20,24},{24,28},{28,32},{32,36}... | collective-permute-start | bytes 1229576 | tf_op jit(solution)/shard_map/ppermute | solution.py:20
  34.6 79.3 %collective-permute-start.5 = (bf16[1,1601,128]{2,1,0:T(8,128)(2,1)S(1)}, bf16[1,1601,128]{2,1,0:T(8,128)(2,1)}, u32[]{:S(2)}, u32[]{:S(2)}) collective-permute-start(bf16[1,1601,128]{2,1,0:T(8,128)(2,1)S(1)} %copy-done.4), channel_id=1, source_target_pairs={{0,12},{4,16},{8,20},{12,24},{16,28},{20,32},{24,36},{28,40},{32,4... | collective-permute-start | bytes 1229576 | tf_op jit(solution)/shard_map/ppermute | solution.py:20
  143.1 0.7 copy-start.3
  150.1 1.4 copy-start.1
  162.9 28.2 %copy-start = (f32[1,1601,128]{2,0,1:T(1,128)S(1)}, f32[1,1601,128]{2,0,1:T(1,128)}, u32[]{:S(2)}) copy-start(f32[1,1601,128]{2,0,1:T(1,128)} %copy.121) | copy-start | bytes 2459140 | tf_op jit(solution)/shard_map/while/body/eval_jaxpr/while
  217.7 1.4 copy-start.1
  231.6 28.2 %copy-start = (f32[1,1601,128]{2,0,1:T(1,128)S(1)}, f32[1,1601,128]{2,0,1:T(1,128)}, u32[]{:S(2)}) copy-start(f32[1,1601,128]{2,0,1:T(1,128)} %copy.121) | copy-start | bytes 2459140 | tf_op jit(solution)/shard_map/while/body/eval_jaxpr/while
  286.4 1.4 copy-start.1
  300.2 28.2 %copy-start = (f32[1,1601,128]{2,0,1:T(1,128)S(1)}, f32[1,1601,128]{2,0,1:T(1,128)}, u32[]{:S(2)}) copy-start(f32[1,1601,128]{2,0,1:T(1,128)} %copy.121) | copy-start | bytes 2459140 | tf_op jit(solution)/shard_map/while/body/eval_jaxpr/while
  355.1 1.4 copy-start.1
  369.0 28.2 %copy-start = (f32[1,1601,128]{2,0,1:T(1,128)S(1)}, f32[1,1601,128]{2,0,1:T(1,128)}, u32[]{:S(2)}) copy-start(f32[1,1601,128]{2,0,1:T(1,128)} %copy.121) | copy-start | bytes 2459140 | tf_op jit(solution)/shard_map/while/body/eval_jaxpr/while
  423.7 7.4 %copy-start.2 = (f32[4,1601,128]{2,0,1:T(4,128)S(1)}, f32[4,1601,128]{2,0,1:T(4,128)}, u32[]{:S(2)}) copy-start(f32[4,1601,128]{2,0,1:T(4,128)} %get-tuple-element.327) | copy-start | bytes 9836548
  425.9 28.5 %collective-permute-start.9 = (bf16[1,1601,128]{2,0,1:T(2,128)(2,1)S(1)}, bf16[1,1601,128]{2,0,1:T(2,128)(2,1)S(1)}, u32[]{:S(2)}, u32[]{:S(2)}) collective-permute-start(bf16[1,1601,128]{2,0,1:T(2,128)(2,1)S(1)} %get-tuple-element.548), channel_id=1, source_target_pairs={{4,0},{8,4},{12,8},{16,12},{20,16},{24,20},{28,24},{32,28},{36,32}... | collective-permute-start | bytes 1229576 | tf_op jit(solution)/shard_map/ppermute | solution.py:20
  427.8 77.1 %collective-permute-start.11 = (bf16[1,1601,128]{2,0,1:T(2,128)(2,1)S(1)}, bf16[1,1601,128]{2,0,1:T(2,128)(2,1)S(1)}, u32[]{:S(2)}, u32[]{:S(2)}) collective-permute-start(bf16[1,1601,128]{2,0,1:T(2,128)(2,1)S(1)} %get-tuple-element.549), channel_id=1, source_target_pairs={{12,0},{16,4},{20,8},{24,12},{28,16},{32,20},{36,24},{40,28},{44,3... | collective-permute-start | bytes 1229576 | tf_op jit(solution)/shard_map/ppermute | solution.py:20
  429.1 104.7 %collective-permute-start.10 = (bf16[1,1601,128]{2,0,1:T(2,128)(2,1)S(1)}, bf16[1,1601,128]{2,0,1:T(2,128)(2,1)S(1)}, u32[]{:S(2)}, u32[]{:S(2)}) collective-permute-start(bf16[1,1601,128]{2,0,1:T(2,128)(2,1)S(1)} %get-tuple-element.550), channel_id=1, source_target_pairs={{8,0},{12,4},{16,8},{20,12},{24,16},{28,20},{32,24},{36,28},{40,32... | collective-permute-start | bytes 1229576 | tf_op jit(solution)/shard_map/ppermute | solution.py:20
  433.9 118.5 %collective-permute-start.6 = (bf16[1,1601,128]{2,0,1:T(2,128)(2,1)S(1)}, bf16[1,1601,128]{2,0,1:T(2,128)(2,1)S(1)}, u32[]{:S(2)}, u32[]{:S(2)}) collective-permute-start(bf16[1,1601,128]{2,0,1:T(2,128)(2,1)S(1)} %get-tuple-element.551), channel_id=1, source_target_pairs={{4,0},{8,4},{12,8},{16,12},{20,16},{24,20},{28,24},{32,28},{36,32}... | collective-permute-start | bytes 1229576 | tf_op jit(solution)/shard_map/ppermute | solution.py:20
  435.8 137.0 %collective-permute-start.8 = (bf16[1,1601,128]{2,0,1:T(2,128)(2,1)S(1)}, bf16[1,1601,128]{2,0,1:T(2,128)(2,1)S(1)}, u32[]{:S(2)}, u32[]{:S(2)}) collective-permute-start(bf16[1,1601,128]{2,0,1:T(2,128)(2,1)S(1)} %get-tuple-element.552), channel_id=1, source_target_pairs={{12,0},{16,4},{20,8},{24,12},{28,16},{32,20},{36,24},{40,28},{44,3... | collective-permute-start | bytes 1229576 | tf_op jit(solution)/shard_map/ppermute | solution.py:20
  454.3 166.2 %collective-permute-start.7 = (bf16[1,1601,128]{2,0,1:T(2,128)(2,1)S(1)}, bf16[1,1601,128]{2,0,1:T(2,128)(2,1)S(1)}, u32[]{:S(2)}, u32[]{:S(2)}) collective-permute-start(bf16[1,1601,128]{2,0,1:T(2,128)(2,1)S(1)} %get-tuple-element.553), channel_id=1, source_target_pairs={{8,0},{12,4},{16,8},{20,12},{24,16},{28,20},{32,24},{36,28},{40,32... | collective-permute-start | bytes 1229576 | tf_op jit(solution)/shard_map/ppermute | solution.py:20
where the time goes:
time: 630 us; the launch traced here: 623 us
  local copies, waits for them, and re-layouts  274 us (43%)
  waiting for transfers between devices  251 us (40%)
  matrix products  43.3 us (7%)
  other arithmetic  23.8 us (4%)
  starting transfers between devices  22.2 us (4%)
  loops' own time  8.52 us (1%)
    ppermute x12, waiting for transfers between devices, from_behind(): return lax.ppermute(block, axis, route)  251 us
    dynamic_update_slice x16, local copies, waits for them, and re-layouts, block_step(): lax.scan(pair_step, zero_rows, (img_keys, img_values, use_row))  226 us
    ppermute x12, starting transfers between devices, from_behind(): return lax.ppermute(block, axis, route)  22.2 us
    dot_general x8, matrix products, pair_out(): jnp.einsum('htj,jd->thd', weights, v_img[:, k_low:k_low + HD], preferred_...  15.6 us
    dynamic_slice x12, local copies, waits for them, and re-layouts, block_forward(): maxima, totals = lax.map(one_stats, (cand_keys, use_row))  14.6 us
  transfers between devices with their start and end apart: 12, of which 9 were waited for; matrix products, arithmetic and copies ran while one was open for 5% of the time, Pallas kernels for 0%

commit v1 on v0

v1 whole, which is shorter than its diff:
```python
import functools

import jax
import jax.numpy as jnp
from jax import lax
from jax.experimental import pallas as pl
from jax.experimental.pallas import tpu as pltpu
from jax.sharding import PartitionSpec as P

HD = 128
BLOCK = 128
STEP = 2
TOK = 1601
TP = 1616
LP = 1664
NH = 8
EARLY = 5
LANES = 2 * BLOCK
CHUNKS = tuple((i * 256, 256) for i in range(6)) + ((1536, 80),)
SLABS = ((0, 816), (816, 800))
LOG2E = 1.4426950408889634
SCALE = HD**-0.5
LOW = -1e30
MESH = pl.DeviceIdType.MESH
OFFSETS = (-2, -1, 1, 2)
bf16 = jnp.bfloat16
f32 = jnp.float32


def mm(a, b):
    return lax.dot_general(a, b, (((1,), (0,)), ((), ())), preferred_element_type=f32)


def mm_nt(a, b):
    return lax.dot_general(a, b, (((1,), (1,)), ((), ())), preferred_element_type=f32)


def kernel(
    q_ref,
    k_ref,
    v_ref,
    refs_ref,
    g_ref,
    att_ref,
    qgrad_ref,
    dk,
    dv,
    qg,
    kp,
    vp,
    vt,
    kt,
    e_s,
    s_s,
    o_s,
    dq_s,
    m_s,
    w_s,
    st_own,
    st_rcv,
    snd,
    rcv,
    dk_prev,
    dv_prev,
    kv_snd,
    kv_rcv,
    msk,
    msk_rcv,
    live,
    q_send,
    q_recv,
    kv_send,
    kv_recv,
    back_send,
    back_recv,
    ret_send,
    ret_recv,
    st_send,
    st_recv,
    msk_send,
    msk_recv,
):
    n = lax.axis_size("ctx")
    me = lax.axis_index("ctx")

    def at(offset):
        return {"ctx": lax.rem(me + (n + offset), n)}

    def remote(src, dst, ssem, rsem, offset):
        return pltpu.make_async_remote_copy(
            src_ref=src,
            dst_ref=dst,
            send_sem=ssem,
            recv_sem=rsem,
            device_id=at(offset),
            device_id_type=MESH,
        )

    def q_copy(h):
        return remote(qg.at[0, h], qg.at[1, h], q_send.at[h], q_recv.at[h], -STEP)

    def kv_copy(i):
        ref = (kp, vp)[i]
        return remote(ref.at[0], ref.at[1], kv_send.at[i], kv_recv.at[i], 1)

    def back_copy(i):
        return remote(kv_snd.at[i], kv_rcv.at[i], back_send.at[i], back_recv.at[i], -1)

    def ret_copy(h, part):
        return remote(
            snd.at[part, h],
            rcv.at[part, h],
            ret_send.at[part, h],
            ret_recv.at[part, h],
            STEP,
        )

    def st_copy(h, block):
        other = 1 - block
        offset = -STEP if block == 0 else STEP
        return remote(
            st_own.at[block, h],
            st_rcv.at[other, h],
            st_send.at[block, h],
            st_recv.at[other, h],
            offset,
        )

    def st_arrival(h, block):
        return remote(
            st_own.at[block, h],
            st_rcv.at[block, h],
            st_send.at[block, h],
            st_recv.at[block, h],
            STEP,
        )

    def msk_copy():
        return remote(msk.at[1], msk_rcv, msk_send.at[0], msk_recv.at[0], -STEP)

    def head_cols(h):
        return pl.ds(pl.multiple_of(h * HD, HD), HD)

    def load_head(h):
        cols = head_cols(h)
        qg[0, h, 0:HD, :] = q_ref[:, cols].T
        qg[0, h, HD : 2 * HD, :] = g_ref[:, cols].T

    def wide(h, part):
        rows = slice(part * HD, (part + 1) * HD)
        return jnp.concatenate([qg[b, h, rows, :] for b in range(2)], 1)

    def turn(img, src, dst):
        for i in range(13):
            size = min(128, TP - i * 128)
            rows = pl.ds(i * 128, size)
            dst[img, 0:HD, rows] = src[img, rows, :].T

    barrier = pltpu.get_barrier_semaphore()
    for e in OFFSETS:
        pl.semaphore_signal(barrier, inc=1, device_id=at(e), device_id_type=MESH)
    for ref, src in ((kp, k_ref), (vp, v_ref)):
        ref[0, pl.ds(TP - 16, 16), :] = jnp.zeros((16, HD), bf16)
        ref[0, 0:TOK, :] = src[0]
    load_head(0)
    named = refs_ref[...]
    for d in range(4):
        hit = (named == me - d) & (me - d >= 0)
        hit = jnp.max(jnp.where(hit, 1.0, 0.0), axis=1, keepdims=True)
        msk[d // 2, d % 2] = jnp.broadcast_to(hit, (8, BLOCK))
    pl.semaphore_wait(barrier, len(OFFSETS))
    q_copy(0).start()
    kv_copy(0).start()
    msk_copy().start()
    kv_copy(1).start()

    def load_rest(h, carry):
        load_head(h)
        q_copy(h).start()
        return carry

    lax.fori_loop(1, NH, load_rest, 0)
    turn(0, vp, vt)
    turn(0, kp, kt)
    for img in range(2):
        vt[img, HD : HD + 16, :] = jnp.ones((16, LP), bf16)
    dk[...] = jnp.zeros_like(dk)
    dv[...] = jnp.zeros_like(dv)
    dk_prev[...] = jnp.zeros_like(dk_prev)
    dv_prev[...] = jnp.zeros_like(dv_prev)
    msk_copy().wait_recv()
    for img in range(2):
        live[img, :, 0:BLOCK] = msk[0, img]
        live[img, :, BLOCK:LANES] = msk_rcv[img]

    def scores(h):
        q_copy(h).wait_recv()
        scaled = wide(h, 0).astype(f32) * (LOG2E * SCALE)
        high = scaled.astype(bf16)
        low = (scaled - high.astype(f32)).astype(bf16)
        both = jnp.concatenate([high, low], 0)
        tops = []
        for img in range(2):
            m = jnp.full((8, LANES), LOW, f32)
            for first, size in CHUNKS:
                rows = pl.ds(first, size)
                k = kp[img, rows, :]
                s = mm(jnp.concatenate([k, k], 1), both)
                if first + size > TOK:
                    row = lax.broadcasted_iota(jnp.int32, (size, LANES), 0)
                    s = jnp.where(row < TOK - first, s, LOW)
                s_s[img, rows, :] = s
                m = jnp.maximum(m, jnp.max(s.reshape(size // 8, 8, LANES), 0))
            m = jnp.max(m, 0, keepdims=True)
            tops.append(jnp.where(live[img, 0:1, :] > 0.5, m, LOW))
        m = jnp.maximum(tops[0], tops[1])
        m_s[h] = m
        o = jnp.zeros((HD + 16, LANES), f32)
        for img in range(2):
            shift = jnp.where(live[img, 0:1, :] > 0.5, m, -LOW)
            for first, size in CHUNKS:
                rows = pl.ds(first, size)
                e = jnp.exp2(s_s[img, rows, :] - shift).astype(bf16)
                e_s[h, img, rows, :] = e
                if img == 0:
                    o = o + mm(vt[img, :, rows], e)
        o_s[h] = o

    def stats(h):
        o = o_s[h] + mm(vt[1, :, 0:TP], e_s[h, 1])
        o_s[h] = o
        total = o[HD : HD + 1]
        some = total > 0.0
        total = jnp.where(some, total, 1.0)
        grads = wide(h, 1).astype(f32)
        delta = jnp.sum(o[0:HD] * grads, axis=0, keepdims=True) / total
        lse = jnp.where(some, m_s[h] + jnp.log(total) * LOG2E, LOW)
        for b in range(2):
            at_b = slice(b * BLOCK, (b + 1) * BLOCK)
            st_own[b, h, 0:1, :] = lse[:, at_b]
            st_own[b, h, 1:2, :] = delta[:, at_b]
        for b in range(2):
            st_copy(h, b).start()

    def merge(h):
        sides = []
        for b in range(2):
            st_arrival(h, b).wait_recv()
        for ref in (st_own, st_rcv):
            lse = jnp.concatenate([ref[b, h, 0:1, :] for b in range(2)], 1)
            delta = jnp.concatenate([ref[b, h, 1:2, :] for b in range(2)], 1)
            sides.append((lse, delta))
        top = jnp.maximum(sides[0][0], sides[1][0])
        parts = [jnp.exp2(lse - top) for lse, delta in sides]
        inverse = 1.0 / (parts[0] + parts[1])
        delta = (parts[0] * sides[0][1] + parts[1] * sides[1][1]) * inverse
        weight = jnp.exp2(m_s[h] - top) * inverse
        w_s[h, 0:1, :] = weight
        w_s[h, 1:2, :] = delta
        o = o_s[h, 0:HD, :] * weight
        o_s[h, 0:HD, :] = o
        snd[0, h] = o[:, BLOCK:LANES].astype(bf16)
        ret_copy(h, 0).start()

    def backward(h, img, dk_to, dv_to):
        w = w_s[h, 0:1, :]
        delta = w_s[h, 1:2, :]
        q = wide(h, 0)
        g = wide(h, 1)
        gw = (g.astype(f32) * w).astype(bf16)
        qw = (q.astype(f32) * w).astype(bf16)
        dq = jnp.zeros((HD, LANES), f32)
        for first, size in SLABS:
            rows = pl.ds(first, size)
            kept = min(size, dk_to.shape[0] - first)
            e = e_s[h, img, rows, :]
            dp = mm(vp[img, rows, :], g)
            ds = (e.astype(f32) * (dp - delta)).astype(bf16)
            dq = dq + mm(kt[img, :, rows], ds)
            dv_to[pl.ds(first, kept), :] += mm_nt(e, gw)[0:kept]
            dk_to[pl.ds(first, kept), :] += mm_nt(ds, qw)[0:kept]
        dq = dq * (w * SCALE)
        if img == 1:
            dq_s[h] = dq
        else:
            dq = dq + dq_s[h]
            dq_s[h] = dq
            snd[1, h] = dq[:, BLOCK:LANES].astype(bf16)
            ret_copy(h, 1).start()

    def each(first, last, *steps):
        def body(h, carry):
            for step in steps:
                step(h)
            return carry

        lax.fori_loop(first, last, body, 0)

    kv_copy(0).wait_recv()
    turn(1, kp, kt)
    each(0, EARLY, scores)
    kv_copy(1).wait_recv()
    turn(1, vp, vt)
    each(0, EARLY, stats)
    each(EARLY, NH, scores, stats)
    each(0, NH, merge, lambda h: backward(h, 1, dk_prev, dv_prev))
    for i, ref in enumerate((dv_prev, dk_prev)):
        kv_snd[i] = ref[...].astype(bf16)
        back_copy(i).start()
    each(0, NH, lambda h: backward(h, 0, dk, dv))

    def finish(h):
        cols = head_cols(h)
        for part, (ref, out) in enumerate(((o_s, att_ref), (dq_s, qgrad_ref))):
            ret_copy(h, part).wait_recv()
            total = ref[h, 0:HD, 0:BLOCK] + rcv[part, h].astype(f32)
            out[:, cols] = total.T.astype(bf16)

    each(0, NH, finish)
    back_copy(0).wait_recv()
    dv[...] = dv[...] + kv_rcv[0, 0:TOK, :].astype(f32)
    back_copy(1).wait_recv()
    dk[...] = (dk[...] + kv_rcv[1, 0:TOK, :].astype(f32)) * SCALE

    def sent(h):
        q_copy(h).wait_send()
        for i in range(2):
            ret_copy(h, i).wait_send()
            st_copy(h, i).wait_send()

    each(0, NH, sent)
    for i in range(2):
        kv_copy(i).wait_send()
        back_copy(i).wait_send()
    msk_copy().wait_send()


def write_back(att, qgrad, dk, dv, att_out, qgrad_out, dk_out, dv_out, sems):
    copies = [
        pltpu.make_async_copy(dk, dk_out.at[:, 0, :], sems.at[0]),
        pltpu.make_async_copy(dv, dv_out.at[:, 0, :], sems.at[1]),
        pltpu.make_async_copy(att, att_out, sems.at[2]),
        pltpu.make_async_copy(qgrad, qgrad_out, sems.at[3]),
    ]
    for copy in copies:
        copy.start()
    for copy in copies:
        copy.wait()


def on_device(queries, keys, values, refs, upstream):
    vmem = pl.BlockSpec(memory_space=pltpu.VMEM)
    anywhere = pl.BlockSpec(memory_space=pl.ANY)
    dma = pltpu.SemaphoreType.DMA
    attended, query_grad, key_grad, value_grad = pl.pallas_call(
        kernel,
        out_shape=[
            pltpu.MemorySpace.VMEM(queries.shape, bf16),
            pltpu.MemorySpace.VMEM(queries.shape, bf16),
            pltpu.MemorySpace.VMEM((TOK, HD), f32),
            pltpu.MemorySpace.VMEM((TOK, HD), f32),
        ],
        in_specs=[vmem] * 5,
        out_specs=[vmem] * 4,
        scratch_shapes=[
            pltpu.VMEM((2, NH, 2 * HD, BLOCK), bf16),
            pltpu.VMEM((2, TP, HD), bf16),
            pltpu.VMEM((2, TP, HD), bf16),
            pltpu.VMEM((2, HD + 16, LP), bf16),
            pltpu.VMEM((2, HD, LP), bf16),
            pltpu.VMEM((NH, 2, TP, LANES), bf16),
            pltpu.VMEM((2, TP, LANES), f32),
            pltpu.VMEM((NH, HD + 16, LANES), f32),
            pltpu.VMEM((NH, HD, LANES), f32),
            pltpu.VMEM((NH, 1, LANES), f32),
            pltpu.VMEM((NH, 2, LANES), f32),
            pltpu.VMEM((2, NH, 2, BLOCK), f32),
            pltpu.VMEM((2, NH, 2, BLOCK), f32),
            pltpu.VMEM((2, NH, HD, BLOCK), bf16),
            pltpu.VMEM((2, NH, HD, BLOCK), bf16),
            pltpu.VMEM((TP, HD), f32),
            pltpu.VMEM((TP, HD), f32),
            pltpu.VMEM((2, TP, HD), bf16),
            pltpu.VMEM((2, TP, HD), bf16),
            pltpu.VMEM((2, 2, 8, BLOCK), f32),
            pltpu.VMEM((2, 8, BLOCK), f32),
            pltpu.VMEM((2, 8, LANES), f32),
            dma((NH,)),
            dma((NH,)),
            dma((2,)),
            dma((2,)),
            dma((2,)),
            dma((2,)),
            dma((2, NH)),
            dma((2, NH)),
            dma((2, NH)),
            dma((2, NH)),
            dma((1,)),
            dma((1,)),
        ],
        compiler_params=pltpu.CompilerParams(
            collective_id=0, has_side_effects=True, vmem_limit_bytes=44 * 2**20
        ),
    )(queries, keys, values, refs, upstream)
    attended, query_grad, key_grad, value_grad = pl.pallas_call(
        write_back,
        out_shape=[
            jax.ShapeDtypeStruct(queries.shape, bf16),
            jax.ShapeDtypeStruct(queries.shape, bf16),
            jax.ShapeDtypeStruct((TOK, 1, HD), f32),
            jax.ShapeDtypeStruct((TOK, 1, HD), f32),
        ],
        in_specs=[vmem] * 4,
        out_specs=[anywhere] * 4,
        scratch_shapes=[dma((4,))],
        compiler_params=pltpu.CompilerParams(vmem_limit_bytes=4 * 2**20),
    )(attended, query_grad, key_grad, value_grad)
    return (
        attended,
        query_grad,
        key_grad.reshape(keys.shape),
        value_grad.reshape(keys.shape),
    )


def solution(mesh):
    return jax.shard_map(
        on_device,
        mesh=mesh,
        in_specs=(
            P(("dp", "ctx"), "tp"),
            P(("dp", "ctx"), None, "tp"),
            P(("dp", "ctx"), None, "tp"),
            P(("dp", "ctx"), None),
            P(("dp", "ctx"), "tp"),
        ),
        out_specs=(
            P(("dp", "ctx"), "tp"),
            P(("dp", "ctx"), "tp"),
            P(("dp", "ctx"), None, "tp"),
            P(("dp", "ctx"), None, "tp"),
        ),
        check_vma=False,
    )
```

time: 630 us -> 69.7 us (0.11)
  the two profiles are of different devices: /device:TPU:166 before, /device:TPU:1 now
where the time goes in v1:
time: 69.7 us; the launch traced here: 69.4 us
  Pallas kernels  64.2 us (92%)
  local copies, waits for them, and re-layouts  4.55 us (7%)
    pallas_call x1, Pallas kernels, on_device(): pl.pallas_call(kernel, out_shape=[pltpu.MemorySpace.VMEM(queries.shape, b...  62.9 us
    unnamed x10, local copies, waits for them, and re-layouts  4.55 us

profile of v1, /device:TPU:1, one launch (start us, length us, event | category | flops | bytes accessed | tf_op | source)
XLA Modules:
  0.0 69.4 jit_solution(134747509946991520)
XLA Ops:
  0.6 0.0 copy-start
  0.6 1.0 %copy-done = bf16[1,1601,128]{2,1,0:T(8,128)(2,1)S(1)} copy-done((bf16[1,1601,128]{2,1,0:T(8,128)(2,1)S(1)}, bf16[1,1601,128]{2,1,0:T(8,128)(2,1)}, u32[]{:S(2)}) %copy-start) | copy-done | bytes 409880
  1.6 0.0 copy-start.1
  1.6 1.0 %copy-done.1 = bf16[1,1601,128]{2,1,0:T(8,128)(2,1)S(1)} copy-done((bf16[1,1601,128]{2,1,0:T(8,128)(2,1)S(1)}, bf16[1,1601,128]{2,1,0:T(8,128)(2,1)}, u32[]{:S(2)}) %copy-start.1) | copy-done | bytes 409880
  2.6 0.0 copy-start.2
  2.6 0.9 %copy-done.2 = bf16[128,1024]{1,0:T(8,128)(2,1)S(1)} copy-done((bf16[128,1024]{1,0:T(8,128)(2,1)S(1)}, bf16[128,1024]{1,0:T(8,128)(2,1)}, u32[]{:S(2)}) %copy-start.2) | copy-done | bytes 262168
  3.6 0.0 copy-start.3
  3.6 0.9 %copy-done.3 = bf16[128,1024]{1,0:T(8,128)(2,1)S(1)} copy-done((bf16[128,1024]{1,0:T(8,128)(2,1)S(1)}, bf16[128,1024]{1,0:T(8,128)(2,1)}, u32[]{:S(2)}) %copy-start.3) | copy-done | bytes 262168
  4.5 0.0 copy-start.4
  4.5 0.7 copy-done.4
  5.2 62.9 %shard_map.84 = (bf16[128,1024]{1,0:T(8,128)(2,1)S(1)}, bf16[128,1024]{1,0:T(8,128)(2,1)S(1)}, f32[1601,128]{1,0:T(8,128)S(1)}, f32[1601,128]{1,0:T(8,128)S(1)}) custom-call(bf16[128,1024]{1,0:T(8,128)(2,1)S(1)} %copy-done.2, bf16[1,1601,128]{2,1,0:T(8,128)(2,1)S(1)} %copy-done, bf16[1,1601,128]{2,1,0:T(8,128)(2,1)S(1)} %copy-done.1, s32[1,4]{1,0:T(1,128)S(1)} %copy-done.4, ...), custom_call_target="tpu_custom_call" | custom-call | tf_op jit(solution)/shard_map/pallas_call | solution.py:355
  68.1 1.4 %shard_map.85 = (bf16[128,1024]{1,0:T(8,128)(2,1)}, bf16[128,1024]{1,0:T(8,128)(2,1)}, f32[1601,1,128]{2,1,0:T(1,128)}, f32[1601,1,128]{2,1,0:T(1,128)}) custom-call(bf16[128,1024]{1,0:T(8,128)(2,1)S(1)} %get-tuple-element.12.att, bf16[128,1024]{1,0:T(8,128)(2,1)S(1)} %get-tuple-element.13.qgrad, f32[1601,128]{1,0:T(8,128)S(1)} %get-tuple-element.14.dk, ...), custom_call_target="tpu_custom_call" | custom-call | tf_op jit(solution)/shard_map/pallas_call | solution.py:405
Async XLA Ops:
  0.6 1.0 %copy-start = (bf16[1,1601,128]{2,1,0:T(8,128)(2,1)S(1)}, bf16[1,1601,128]{2,1,0:T(8,128)(2,1)}, u32[]{:S(2)}) copy-start(bf16[1,1601,128]{2,1,0:T(8,128)(2,1)} %k_ref.1) | copy-start | bytes 1229572
  1.6 1.0 %copy-start.1 = (bf16[1,1601,128]{2,1,0:T(8,128)(2,1)S(1)}, bf16[1,1601,128]{2,1,0:T(8,128)(2,1)}, u32[]{:S(2)}) copy-start(bf16[1,1601,128]{2,1,0:T(8,128)(2,1)} %v_ref.1) | copy-start | bytes 1229572
  2.6 0.9 %copy-start.2 = (bf16[128,1024]{1,0:T(8,128)(2,1)S(1)}, bf16[128,1024]{1,0:T(8,128)(2,1)}, u32[]{:S(2)}) copy-start(bf16[128,1024]{1,0:T(8,128)(2,1)} %q_ref.1) | copy-start | bytes 786436
  3.6 0.9 %copy-start.3 = (bf16[128,1024]{1,0:T(8,128)(2,1)S(1)}, bf16[128,1024]{1,0:T(8,128)(2,1)}, u32[]{:S(2)}) copy-start(bf16[128,1024]{1,0:T(8,128)(2,1)} %g_ref.1) | copy-start | bytes 786436
  4.5 0.7 copy-start.4

commit v2 on v1

v2 whole, which is shorter than its diff:
```python
import functools

import jax
import jax.numpy as jnp
from jax import lax
from jax.experimental import pallas as pl
from jax.experimental.pallas import tpu as pltpu
from jax.sharding import PartitionSpec as P

HD = 128
BLOCK = 128
STEP = 2
TOK = 1601
TP = 1616
LP = 1664
NH = 8
PAIRS = NH // 2
LANES = 4 * BLOCK
CHUNKS = tuple((i * 256, 256) for i in range(6)) + ((1536, 80),)
ORDER = ((0, 0), (0, 1), (1, 0), (1, 1))
LOG2E = 1.4426950408889634
SCALE = HD**-0.5
LOW = -1e30
MESH = pl.DeviceIdType.MESH
OFFSETS = (-2, -1, 1, 2)
bf16 = jnp.bfloat16
f32 = jnp.float32


def mm(a, b):
    return lax.dot_general(a, b, (((1,), (0,)), ((), ())), preferred_element_type=f32)


def mm_nt(a, b):
    return lax.dot_general(a, b, (((1,), (1,)), ((), ())), preferred_element_type=f32)


def kernel(
    q_ref,
    k_ref,
    v_ref,
    refs_ref,
    g_ref,
    att_ref,
    qgrad_ref,
    dk,
    dv,
    rows_in,
    tokens_in,
    refs_in,
    qg,
    kp,
    vp,
    vt,
    kt,
    e_s,
    s_s,
    o_s,
    dq_s,
    m_s,
    l_s,
    w_s,
    d_s,
    lse_own,
    lse_rcv,
    del_own,
    del_rcv,
    snd,
    rcv,
    dk_prev,
    dv_prev,
    kv_snd,
    kv_rcv,
    msk,
    msk_rcv,
    live,
    in_sem,
    q_send,
    q_recv,
    kv_send,
    kv_recv,
    back_send,
    back_recv,
    ret_send,
    ret_recv,
    lse_send,
    lse_recv,
    del_send,
    del_recv,
    msk_send,
    msk_recv,
):
    n = lax.axis_size("ctx")
    me = lax.axis_index("ctx")

    def at(offset):
        return {"ctx": lax.rem(me + (n + offset), n)}

    def remote(src, dst, ssem, rsem, offset):
        return pltpu.make_async_remote_copy(
            src_ref=src,
            dst_ref=dst,
            send_sem=ssem,
            recv_sem=rsem,
            device_id=at(offset),
            device_id_type=MESH,
        )

    def q_copy(p, part):
        heads = pl.ds(2 * p, 2)
        return remote(
            qg.at[0, part, heads],
            qg.at[1, part, heads],
            q_send.at[part, p],
            q_recv.at[part, p],
            -STEP,
        )

    def kv_copy(i):
        ref = (kp, vp)[i]
        return remote(ref.at[0], ref.at[1], kv_send.at[i], kv_recv.at[i], 1)

    def back_copy(i):
        return remote(kv_snd.at[i], kv_rcv.at[i], back_send.at[i], back_recv.at[i], -1)

    def ret_copy(p, part):
        return remote(
            snd.at[part, p],
            rcv.at[part, p],
            ret_send.at[part, p],
            ret_recv.at[part, p],
            STEP,
        )

    def swap(own, taken, ssem, rsem, p, block):
        return remote(
            own.at[block, p],
            taken.at[1 - block, p],
            ssem.at[block, p],
            rsem.at[1 - block, p],
            -STEP if block == 0 else STEP,
        )

    def swapped(own, taken, ssem, rsem, p, block):
        return remote(
            own.at[block, p],
            taken.at[block, p],
            ssem.at[block, p],
            rsem.at[block, p],
            STEP,
        )

    lse_refs = (lse_own, lse_rcv, lse_send, lse_recv)
    del_refs = (del_own, del_rcv, del_send, del_recv)

    def give(refs, p, row):
        for i, (j, b) in enumerate(ORDER):
            refs[0][b, p, j : j + 1, :] = row[:, i * BLOCK : (i + 1) * BLOCK]
        for b in range(2):
            swap(*refs, p, b).start()

    def take(refs, p):
        for b in range(2):
            swapped(*refs, p, b).wait_recv()
        return [
            jnp.concatenate([r[b, p, j : j + 1, :] for j, b in ORDER], 1)
            for r in refs[:2]
        ]

    def msk_copy():
        return remote(msk.at[1], msk_rcv, msk_send.at[0], msk_recv.at[0], -STEP)

    def each(first, last, *steps):
        def body(i, carry):
            for step in steps:
                step(i)
            return carry

        lax.fori_loop(first, last, body, 0)

    def head_cols(h):
        return pl.ds(pl.multiple_of(h * HD, HD), HD)

    def load_head(h, part):
        qg[0, part, h] = rows_in[part, :, head_cols(h)].T

    def wide(p, part):
        return jnp.concatenate([qg[b, part, 2 * p + j] for j, b in ORDER], 1)

    def turn(img, src, dst):
        for i in range(13):
            size = min(128, TP - i * 128)
            rows = pl.ds(i * 128, size)
            dst[img, :, rows] = src[img, rows, :].T

    loads = [
        pltpu.make_async_copy(q_ref, rows_in.at[0], in_sem.at[0]),
        pltpu.make_async_copy(k_ref.at[0], tokens_in.at[0], in_sem.at[1]),
        pltpu.make_async_copy(v_ref.at[0], tokens_in.at[1], in_sem.at[2]),
        pltpu.make_async_copy(refs_ref, refs_in, in_sem.at[3]),
        pltpu.make_async_copy(g_ref, rows_in.at[1], in_sem.at[4]),
    ]
    for load in loads:
        load.start()
    barrier = pltpu.get_barrier_semaphore()
    for e in OFFSETS:
        pl.semaphore_signal(barrier, inc=1, device_id=at(e), device_id_type=MESH)
    dk[...] = jnp.zeros_like(dk)
    dv[...] = jnp.zeros_like(dv)
    dk_prev[...] = jnp.zeros_like(dk_prev)
    dv_prev[...] = jnp.zeros_like(dv_prev)
    for load in loads:
        load.wait()
    for i, ref in enumerate((kp, vp)):
        ref[0, pl.ds(TP - 16, 16), :] = jnp.zeros((16, HD), bf16)
        ref[0, 0:TOK, :] = tokens_in[i]
    named = refs_in[...]
    for d in range(4):
        hit = (named == me - d) & (me - d >= 0)
        hit = jnp.max(jnp.where(hit, 1.0, 0.0), axis=1, keepdims=True)
        msk[d // 2, d % 2] = jnp.broadcast_to(hit, (8, BLOCK))
    for h in range(NH):
        load_head(h, 0)
    pl.semaphore_wait(barrier, len(OFFSETS))
    q_copy(0, 0).start()
    kv_copy(0).start()
    msk_copy().start()
    for p in range(1, PAIRS):
        q_copy(p, 0).start()
    kv_copy(1).start()
    for p in range(PAIRS):
        load_head(2 * p, 1)
        load_head(2 * p + 1, 1)
    turn(0, vp, vt)
    turn(0, kp, kt)
    msk_copy().wait_recv()
    for img in range(2):
        for i, (j, b) in enumerate(ORDER):
            src = msk[0, img] if b == 0 else msk_rcv[img]
            live[img, :, i * BLOCK : (i + 1) * BLOCK] = src

    def scores(p, img):
        scaled = wide(p, 0).astype(f32) * (LOG2E * SCALE)
        high = scaled.astype(bf16)
        low = (scaled - high.astype(f32)).astype(bf16)
        both = jnp.concatenate([high, low], 0)
        m = jnp.full((8, LANES), LOW, f32)
        for first, size in CHUNKS:
            rows = pl.ds(first, size)
            k = kp[img, rows, :]
            s = mm(jnp.concatenate([k, k], 1), both)
            if first + size > TOK:
                row = lax.broadcasted_iota(jnp.int32, (size, LANES), 0)
                s = jnp.where(row < TOK - first, s, LOW)
            s_s[rows, :] = s
            m = jnp.maximum(m, jnp.max(s.reshape(size // 8, 8, LANES), 0))
        m = jnp.max(m, 0, keepdims=True)
        total = jnp.zeros((8, LANES), f32)
        o = jnp.zeros((HD, LANES), f32)
        for first, size in CHUNKS:
            rows = pl.ds(first, size)
            e = jnp.exp2(s_s[rows, :] - m)
            total = total + jnp.sum(e.reshape(size // 8, 8, LANES), 0)
            e = e.astype(bf16)
            e_s[p, img, rows, :] = e
            if img == 0:
                o = o + mm(vt[img, :, rows], e)
        if img == 0:
            o_s[p] = o
        m_s[p, img] = jnp.where(live[img, 0:1, :] > 0.5, m, LOW)
        l_s[p, img] = jnp.sum(total, 0, keepdims=True)

    def scores_own(p):
        q_copy(p, 0).wait_recv()
        scores(p, 0)

        @pl.when(p == 1)
        def _():
            q_copy(0, 1).start()

    def scores_prev(p):
        scores(p, 1)
        m = [m_s[p, img] for img in range(2)]
        top = jnp.maximum(m[0], m[1])
        total = sum(l_s[p, img] * jnp.exp2(m[img] - top) for img in range(2))
        give(lse_refs, p, top + jnp.log(total) * LOG2E)

        @pl.when(p + 1 < PAIRS)
        def _():
            q_copy(p + 1, 1).start()

    def merge(p):
        lses = take(lse_refs, p)
        top = jnp.maximum(lses[0], lses[1])
        inverse = 1.0 / (jnp.exp2(lses[0] - top) + jnp.exp2(lses[1] - top))
        for img in range(2):
            w_s[p, img] = jnp.exp2(m_s[p, img] - top) * inverse

    def values_back(p, img, dv_to):
        kept = dv_to.shape[0]
        gw = (wide(p, 1).astype(f32) * w_s[p, img]).astype(bf16)
        dv_to[...] += mm_nt(e_s[p, img], gw)[0:kept]

    def values_prev(p):
        merge(p)
        q_copy(p, 1).wait_recv()
        values_back(p, 1, dv_prev)

    def send_parts(p, part, total):
        for j in range(2):
            low = (2 * j + 1) * BLOCK
            snd[part, p, j] = total[:, low : low + BLOCK].astype(bf16)
        ret_copy(p, part).start()

    def outputs(p):
        o = o_s[p] * w_s[p, 0] + mm(vt[1, :, 0:TP], e_s[p, 1]) * w_s[p, 1]
        o_s[p] = o
        give(del_refs, p, jnp.sum(o * wide(p, 1).astype(f32), axis=0, keepdims=True))

    def send_output(p):
        send_parts(p, 0, o_s[p])

    def backward(p, img, dk_to):
        w = w_s[p, img]
        delta = d_s[p]
        kept = dk_to.shape[0]
        qw = (wide(p, 0).astype(f32) * w).astype(bf16)
        dp = mm(vp[img], wide(p, 1))
        ds = (e_s[p, img].astype(f32) * (dp - delta)).astype(bf16)
        dk_to[...] += mm_nt(ds, qw)[0:kept]
        return mm(kt[img, :, 0:TP], ds) * (w * SCALE)

    def backward_prev(p):
        deltas = take(del_refs, p)
        d_s[p] = deltas[0] + deltas[1]
        dq_s[p] = backward(p, 1, dk_prev)

    def backward_own(p):
        dq = backward(p, 0, dk) + dq_s[p]
        dq_s[p] = dq
        send_parts(p, 1, dq)

    def values_own(p):
        values_back(p, 0, dv)

    def backward_next(p):
        backward_prev(p + 1)

    def send_back(i, ref):
        kv_snd[i] = ref[...].astype(bf16)
        back_copy(i).start()

    last = PAIRS - 1
    each(0, last, scores_own)
    kv_copy(0).wait_recv()
    each(0, last, scores_prev)
    scores_own(last)
    scores_prev(last)
    turn(1, kp, kt)
    values_prev(0)
    values_prev(1)
    kv_copy(1).wait_recv()
    turn(1, vp, vt)
    outputs(0)
    outputs(1)
    send_output(0)
    values_prev(2)
    outputs(2)
    send_output(1)
    backward_prev(0)
    values_prev(last)
    outputs(last)
    send_back(0, dv_prev)
    each(2, PAIRS, send_output)
    each(0, 2, backward_own, backward_next)
    backward_prev(last)
    send_back(1, dk_prev)
    each(2, PAIRS, backward_own)
    each(0, PAIRS, values_own)

    def finish(part):
        ref, out = ((o_s, att_ref), (dq_s, qgrad_ref))[part]

        def step(p):
            ret_copy(p, part).wait_recv()
            for j in range(2):
                total = ref[p, :, 2 * j * BLOCK : (2 * j + 1) * BLOCK]
                total = total + rcv[part, p, j].astype(f32)
                out[:, head_cols(2 * p + j)] = total.T.astype(bf16)

        return step

    each(0, PAIRS, finish(0))
    back_copy(0).wait_recv()
    dv[...] = dv[...] + kv_rcv[0, 0:TOK, :].astype(f32)
    each(0, PAIRS, finish(1))
    back_copy(1).wait_recv()
    dk[...] = (dk[...] + kv_rcv[1, 0:TOK, :].astype(f32)) * SCALE

    def sent(p):
        for i in range(2):
            q_copy(p, i).wait_send()
            ret_copy(p, i).wait_send()
            swap(*lse_refs, p, i).wait_send()
            swap(*del_refs, p, i).wait_send()

    each(0, PAIRS, sent)
    for i in range(2):
        kv_copy(i).wait_send()
        back_copy(i).wait_send()
    msk_copy().wait_send()


def write_back(att, qgrad, dk, dv, att_out, qgrad_out, dk_out, dv_out, sems):
    copies = [
        pltpu.make_async_copy(dk, dk_out.at[:, 0, :], sems.at[0]),
        pltpu.make_async_copy(dv, dv_out.at[:, 0, :], sems.at[1]),
        pltpu.make_async_copy(att, att_out, sems.at[2]),
        pltpu.make_async_copy(qgrad, qgrad_out, sems.at[3]),
    ]
    for copy in copies:
        copy.start()
    for copy in copies:
        copy.wait()


def on_device(queries, keys, values, refs, upstream):
    vmem = pl.BlockSpec(memory_space=pltpu.VMEM)
    anywhere = pl.BlockSpec(memory_space=pl.ANY)
    dma = pltpu.SemaphoreType.DMA
    hbm = pltpu.MemorySpace.HBM
    queries, keys, values, refs, upstream = (
        pltpu.with_memory_space_constraint(x, hbm)
        for x in (queries, keys, values, refs, upstream)
    )
    attended, query_grad, key_grad, value_grad = pl.pallas_call(
        kernel,
        out_shape=[
            pltpu.MemorySpace.VMEM(queries.shape, bf16),
            pltpu.MemorySpace.VMEM(queries.shape, bf16),
            pltpu.MemorySpace.VMEM((TOK, HD), f32),
            pltpu.MemorySpace.VMEM((TOK, HD), f32),
        ],
        in_specs=[pl.BlockSpec(memory_space=hbm)] * 5,
        out_specs=[vmem] * 4,
        scratch_shapes=[
            pltpu.VMEM((2, BLOCK, NH * HD), bf16),
            pltpu.VMEM((2, TOK, HD), bf16),
            pltpu.VMEM((1, 4), jnp.int32),
            pltpu.VMEM((2, 2, NH, HD, BLOCK), bf16),
            pltpu.VMEM((2, TP, HD), bf16),
            pltpu.VMEM((2, TP, HD), bf16),
            pltpu.VMEM((2, HD, LP), bf16),
            pltpu.VMEM((2, HD, LP), bf16),
            pltpu.VMEM((PAIRS, 2, TP, LANES), bf16),
            pltpu.VMEM((TP, LANES), f32),
            pltpu.VMEM((PAIRS, HD, LANES), f32),
            pltpu.VMEM((PAIRS, HD, LANES), f32),
            pltpu.VMEM((PAIRS, 2, 1, LANES), f32),
            pltpu.VMEM((PAIRS, 2, 1, LANES), f32),
            pltpu.VMEM((PAIRS, 2, 1, LANES), f32),
            pltpu.VMEM((PAIRS, 1, LANES), f32),
            pltpu.VMEM((2, PAIRS, 2, BLOCK), f32),
            pltpu.VMEM((2, PAIRS, 2, BLOCK), f32),
            pltpu.VMEM((2, PAIRS, 2, BLOCK), f32),
            pltpu.VMEM((2, PAIRS, 2, BLOCK), f32),
            pltpu.VMEM((2, PAIRS, 2, HD, BLOCK), bf16),
            pltpu.VMEM((2, PAIRS, 2, HD, BLOCK), bf16),
            pltpu.VMEM((TP, HD), f32),
            pltpu.VMEM((TP, HD), f32),
            pltpu.VMEM((2, TP, HD), bf16),
            pltpu.VMEM((2, TP, HD), bf16),
            pltpu.VMEM((2, 2, 8, BLOCK), f32),
            pltpu.VMEM((2, 8, BLOCK), f32),
            pltpu.VMEM((2, 8, LANES), f32),
            dma((5,)),
            dma((2, PAIRS)),
            dma((2, PAIRS)),
            dma((2,)),
            dma((2,)),
            dma((2,)),
            dma((2,)),
            dma((2, PAIRS)),
            dma((2, PAIRS)),
            dma((2, PAIRS)),
            dma((2, PAIRS)),
            dma((2, PAIRS)),
            dma((2, PAIRS)),
            dma((1,)),
            dma((1,)),
        ],
        compiler_params=pltpu.CompilerParams(
            collective_id=0, has_side_effects=True, vmem_limit_bytes=48 * 2**20
        ),
    )(queries, keys, values, refs, upstream)
    attended, query_grad, key_grad, value_grad = pl.pallas_call(
        write_back,
        out_shape=[
            jax.ShapeDtypeStruct(queries.shape, bf16),
            jax.ShapeDtypeStruct(queries.shape, bf16),
            jax.ShapeDtypeStruct((TOK, 1, HD), f32),
            jax.ShapeDtypeStruct((TOK, 1, HD), f32),
        ],
        in_specs=[vmem] * 4,
        out_specs=[anywhere] * 4,
        scratch_shapes=[dma((4,))],
        compiler_params=pltpu.CompilerParams(vmem_limit_bytes=4 * 2**20),
    )(attended, query_grad, key_grad, value_grad)
    return (
        attended,
        query_grad,
        key_grad.reshape(keys.shape),
        value_grad.reshape(keys.shape),
    )


def solution(mesh):
    return jax.shard_map(
        on_device,
        mesh=mesh,
        in_specs=(
            P(("dp", "ctx"), "tp"),
            P(("dp", "ctx"), None, "tp"),
            P(("dp", "ctx"), None, "tp"),
            P(("dp", "ctx"), None),
            P(("dp", "ctx"), "tp"),
        ),
        out_specs=(
            P(("dp", "ctx"), "tp"),
            P(("dp", "ctx"), "tp"),
            P(("dp", "ctx"), None, "tp"),
            P(("dp", "ctx"), None, "tp"),
        ),
        check_vma=False,
    )
```

time: 69.7 us -> 62.1 us (0.89)
  local copies, waits for them, and re-layouts: 4.55 us -> 0 us
  Pallas kernels: 64.2 us -> 60.8 us
    unnamed x10 -> x0, local copies, waits for them, and re-layouts: 4.55 us -> none
    pallas_call x1, Pallas kernels: 62.9 us -> 59.5 us  [on_device(): pl.pallas_call(kernel, out_shape=[pltpu.MemorySpace.VMEM(queries.shape, b...]
where the time goes in v2:
time: 62.1 us; the launch traced here: 61.6 us
  Pallas kernels  60.8 us (98%)
  between operations  0.8 us (1%)
    pallas_call x1, Pallas kernels, on_device(): pl.pallas_call(kernel, out_shape=[pltpu.MemorySpace.VMEM(queries.shape, b...  59.5 us
    pallas_call x1, Pallas kernels, on_device(): pl.pallas_call(write_back, out_shape=[jax.ShapeDtypeStruct(queries.shape,...  1.37 us

profile of v2, /device:TPU:1, one launch (start us, length us, event | category | flops | bytes accessed | tf_op | source)
XLA Modules:
  0.0 61.6 jit_solution(5784014921026893749)
XLA Ops:
  0.6 59.5 %shard_map.84 = (bf16[128,1024]{1,0:T(8,128)(2,1)S(1)}, bf16[128,1024]{1,0:T(8,128)(2,1)S(1)}, f32[1601,128]{1,0:T(8,128)S(1)}, f32[1601,128]{1,0:T(8,128)S(1)}) custom-call(bf16[128,1024]{1,0:T(8,128)(2,1)} %q_ref.1, bf16[1,1601,128]{2,1,0:T(8,128)(2,1)} %k_ref.1, bf16[1,1601,128]{2,1,0:T(8,128)(2,1)} %v_ref.1, s32[1,4]{1,0:T(1,128)} %refs_ref.1, ...), custom_call_target="tpu_custom_call" | custom-call | tf_op jit(solution)/shard_map/pallas_call | solution.py:436
  60.1 1.4 %shard_map.85 = (bf16[128,1024]{1,0:T(8,128)(2,1)}, bf16[128,1024]{1,0:T(8,128)(2,1)}, f32[1601,1,128]{2,1,0:T(1,128)}, f32[1601,1,128]{2,1,0:T(1,128)}) custom-call(bf16[128,1024]{1,0:T(8,128)(2,1)S(1)} %get-tuple-element.12.att, bf16[128,1024]{1,0:T(8,128)(2,1)S(1)} %get-tuple-element.13.qgrad, f32[1601,128]{1,0:T(8,128)S(1)} %get-tuple-element.14.dk, ...), custom_call_target="tpu_custom_call" | custom-call | tf_op jit(solution)/shard_map/pallas_call | solution.py:496
